TPU v7x, 32 devices: a whole 2x2x4 slice. The times are simulated.
32 devices in a mesh: blk: 16 (over z, x, core), rep: 2 (over y).
Axes of the slice: x: 2, y: 2, z: 4, core: 2. Of those that a mesh axis runs over, the one named last changes fastest.
Arguments:
- features: bfloat16 [4096, 256], P('blk'), may hold values from -6 to 6
- degree: int32 [4096], P('blk'), may hold values from 1 to 4
- tiles: bfloat16 [16, 2, 16, 8, 128, 128], P('blk', 'rep'), may hold values from -0.0625 to 0.0625
- block_rows: int32 [16, 2, 16, 8], P('blk', 'rep'), may hold values from 0 to 1
- block_cols: int32 [16, 2, 16, 8], P('blk', 'rep'), may hold values from 0 to 1
- live: int32 [16, 2, 16], P('blk', 'rep'), may hold values from 1 to 8, as said below
- w_self: bfloat16 [256, 256], replicated, may hold values from -0.375 to 0.375
- w_neigh: bfloat16 [256, 256], replicated, may hold values from -0.375 to 0.375
- bias: float32 [256], replicated, may hold values from -3 to 3
- cotangent: bfloat16 [4096, 256], P('blk'), may hold values from -1 to 1
Outputs:
- hidden_out: bfloat16 [4096, 256], P(('blk', 'rep'))
- feature_grad: bfloat16 [4096, 256], P(('blk', 'rep'))
- grad_self: float32 [256, 256], replicated
- grad_neigh: float32 [256, 256], replicated
- grad_bias: float32 [256], replicated
Inputs may be any that keep to these rules, and one draw needn't show every extreme that they name: `live`: each device's slots for one column slab are used from slot 0 on; at most 8, and exactly 8 for some device and slab.
All inputs are finite; a program needn't handle non-finite values.
Results may differ from a plain program's by a relative error of at most 0.0095.
Values may be sent and summed in bfloat16 or wider, within the bound.
A program may use at most 192 MiB of HBM per device.

v0:
```python
import jax
import jax.numpy as jnp
from jax import lax
from jax.sharding import PartitionSpec as P


def silu_slope(pre):
    sig = jax.nn.sigmoid(pre)
    return sig * (1.0 + pre * (1.0 - sig))


def window_slabs(count, slab, nslab):
    return min(count // slab, nslab)


def slot_offsets(first, m, cols, live, slab, tile):
    cap = cols.shape[1]
    slab_ids = first + jnp.arange(m, dtype=jnp.int32)
    offset = slab_ids[:, None] * slab + cols * tile
    used = jnp.arange(cap, dtype=jnp.int32)[None, :] < live[:, None]
    return (offset.reshape(m * cap), used.reshape(m * cap))


def block_table(offset, used, tile, count):
    nparts = count // tile
    valid = used & (offset >= 0) & (offset < count)
    target = jnp.where(offset >= 0, offset, 0) // tile
    return (target[:, None] == jnp.arange(nparts, dtype=jnp.int32)[None, :]) & valid[:, None]


def shards(features, degree, tiles, block_rows, block_cols, live, w_self, w_neigh, bias, cotangent):
    tiles = tiles[0, 0]
    rows = block_rows[0, 0]
    cols = block_cols[0, 0]
    live = live[0, 0]
    nslab = tiles.shape[0]
    cap = tiles.shape[1]
    tile = tiles.shape[2]
    slab, width = features.shape
    nblock = slab // tile
    share = slab // lax.axis_size("rep")
    mine = lax.axis_index("rep") * share
    block_ids = jnp.arange(nblock, dtype=jnp.int32)
    piece = lax.all_gather(features, "blk", axis=0, tiled=True)
    count = piece.shape[0]
    m = window_slabs(count, slab, nslab)
    first = jnp.clip(jnp.int32(0) // slab, 0, nslab - m)
    offset, used = slot_offsets(first, m, cols, live, slab, tile)
    select = block_table(offset, used, tile, count).astype(jnp.bfloat16)
    picked = jnp.einsum(
        "tb,bif->tif",
        select,
        piece.reshape(count // tile, tile, width),
        preferred_element_type=jnp.float32,
    ).astype(jnp.bfloat16)
    tile_sel = tiles.reshape(m * cap, tile, tile)
    prods = jnp.einsum("tij,tjf->tif", tile_sel, picked, preferred_element_type=jnp.float32)
    row_sel = rows.reshape(-1)
    onehot = (row_sel[:, None] == block_ids[None, :]).astype(jnp.float32)
    added = jnp.einsum("tb,tif->bif", onehot, prods, precision=lax.Precision.HIGHEST)
    partial_value = added.reshape(slab, width)
    degf = degree.astype(jnp.float32)[:, None]
    agg_sum = lax.psum_scatter(partial_value, "rep", scatter_dimension=0, tiled=True)
    x_mine = lax.dynamic_slice_in_dim(features, mine, share, 0)
    deg_mine = lax.dynamic_slice_in_dim(degf, mine, share, 0)
    cot_mine = lax.dynamic_slice_in_dim(cotangent, mine, share, 0)
    agg = (agg_sum / deg_mine).astype(jnp.bfloat16)
    pre = (
        jnp.dot(x_mine, w_self, preferred_element_type=jnp.float32)
        + jnp.dot(agg, w_neigh, preferred_element_type=jnp.float32)
        + bias
    )
    hidden_out = jax.nn.silu(pre).astype(jnp.bfloat16)
    dpre = (cot_mine.astype(jnp.float32) * silu_slope(pre)).astype(jnp.bfloat16)
    dagg = (
        jnp.einsum("ne,de->nd", dpre, w_neigh, preferred_element_type=jnp.float32) / deg_mine
    ).astype(jnp.bfloat16)
    dagg_slab = lax.all_gather(dagg, "rep", axis=0, tiled=True)
    grad_self, grad_neigh, grad_bias = lax.psum(
        (
            jnp.einsum("nd,ne->de", x_mine, dpre, preferred_element_type=jnp.float32),
            jnp.einsum("nd,ne->de", agg, dpre, preferred_element_type=jnp.float32),
            jnp.sum(dpre.astype(jnp.float32), axis=0),
        ),
        ("blk", "rep"),
    )
    grad_blocks = dagg_slab.reshape(nblock, tile, width)
    count = slab * lax.axis_size("blk")
    m = window_slabs(count, slab, nslab)
    first = jnp.clip(jnp.int32(0) // slab, 0, nslab - m)
    offset, used = slot_offsets(first, m, cols, live, slab, tile)
    tile_sel = tiles.reshape(m * cap, tile, tile)
    row_sel = rows.reshape(-1)
    row_onehot = (row_sel[:, None] == block_ids[None, :]).astype(jnp.bfloat16)
    picked = jnp.einsum(
        "tb,bjf->tjf", row_onehot, grad_blocks, preferred_element_type=jnp.float32
    ).astype(jnp.bfloat16)
    prods = jnp.einsum("tji,tjf->tif", tile_sel, picked, preferred_element_type=jnp.float32)
    select = block_table(offset, used, tile, count).astype(jnp.float32)
    added = jnp.einsum("tb,tif->bif", select, prods, precision=lax.Precision.HIGHEST)
    slab_part = lax.psum_scatter(
        added.reshape(count, width).astype(jnp.bfloat16), "blk", scatter_dimension=0, tiled=True
    )
    neigh_part = lax.psum_scatter(slab_part, "rep", scatter_dimension=0, tiled=True).astype(
        jnp.float32
    )
    self_part = jnp.einsum("ne,de->nd", dpre, w_self, preferred_element_type=jnp.float32)
    feature_grad = (self_part + neigh_part).astype(jnp.bfloat16)
    return (hidden_out, feature_grad, grad_self, grad_neigh, grad_bias)


def solution(mesh):
    return jax.shard_map(
        shards,
        mesh=mesh,
        in_specs=(
            P("blk", None),
            P("blk"),
            P("blk", "rep", None, None, None, None),
            P("blk", "rep", None, None),
            P("blk", "rep", None, None),
            P("blk", "rep", None),
            P(),
            P(),
            P(),
            P("blk", None),
        ),
        out_specs=(P(("blk", "rep"), None), P(("blk", "rep"), None), P(), P(), P()),
        check_vma=False,
    )
```

profile of v0, /device:TPU:0, one launch (start us, length us, event | category | flops | bytes accessed | tf_op | source)
XLA Modules:
  0.0 392.6 jit_solution(15062594691066460725)
XLA Ops:
  7.2 0.0 copy-start
  7.2 0.0 all-gather.2.cloned.1.call-start
  7.2 0.7 all-gather.2.cloned.1.call-update
  7.9 0.0 reduce-scatter.4.cloned.1.call-start
  8.0 0.1 add.73
  8.0 0.1 add.74
  8.1 0.7 broadcast_multiply_fusion
  8.8 0.1 copy.19
  8.9 0.1 mul.43
  9.0 0.7 iota_compare_fusion.1
  9.7 0.1 lt.48
  9.8 0.8 copy.18
  10.6 0.1 eq.14
  10.7 43.6 %all-gather.2.cloned.1.call-done = bf16[4096,256]{1,0:T(8,128)(2,1)} async-done(((bf16[256,256]{1,0:T(8,128)(2,1)}), bf16[4096,256]{1,0:T(8,128)(2,1)}) %all-gather.2.cloned.1.call-update) | async-done | bytes 2097168 | tf_op jit(solution)/shard_map/all_gather | solution.py:44
  54.3 7.2 %fusion.6 = bf16[128,128,256]{2,0,1:T(8,128)(2,1)} fusion(bf16[32,128,256]{2,1,0:T(8,128)(2,1)} %bitcast.40, s32[128]{0:T(128)S(1)} %and_select_fusion, pred[128]{0:T(512)(128)(4,1)S(1)} %fusion.28), kind=kOutput, calls=%fused_computation.8 | convolution fusion | flops 268443648 | bytes 10486400 | tf_op jit(solution)/shard_map/tb,bif->tif/dot_general | solution.py:50
  61.5 16.5 %fusion.4 = f32[128,256,128]{2,1,0:T(8,128)} fusion(bf16[128,128,128]{2,1,0:T(8,128)(2,1)} %bitcast.37, bf16[128,128,256]{2,0,1:T(8,128)(2,1)} %fusion.6), kind=kOutput, calls=%fused_computation.6 | convolution fusion | flops 1073741824 | bytes 29360128 | tf_op jit(solution)/shard_map/tij,tjf->tif/dot_general | solution.py:57
  78.0 17.7 %copy.24 = f32[128,256,128]{1,0,2:T(8,128)} copy(f32[128,256,128]{2,1,0:T(8,128)} %fusion.4) | data formatting | bytes 33554432 | tf_op jit(solution)/shard_map/tij,tjf->tif/dot_general | solution.py:57
  95.7 0.0 copy-start.4
  95.7 0.0 copy-start.2
  95.7 0.0 copy-start.3
  95.7 0.0 copy-start.5
  95.8 0.0 copy-start.7
  95.8 9.1 %fusion.2 = f32[2,128,256]{2,0,1:T(2,128)S(1)} fusion(f32[128,256,128]{1,0,2:T(8,128)} %copy.24, s32[128]{0:T(128)S(1)} %eq.14), kind=kOutput, calls=%fused_computation.2 | convolution fusion | flops 100663552 | bytes 17039872 | tf_op jit(solution)/shard_map/tb,tif->bif/dot_general | solution.py:60
  104.9 0.7 copy.20
  105.6 0.0 reduce-scatter.4.cloned.1.call-update
  105.6 0.2 reduce-scatter.6.cloned.1.call-start
  105.8 0.0 copy-done.4
  105.9 0.1 dynamic-slice.3
  105.9 0.0 copy-done.2
  105.9 0.0 copy-done.3
  105.9 0.2 fusion.18
  106.1 10.1 %reduce-scatter.4.cloned.1.call-done = f32[128,256]{1,0:T(8,128)} async-done(((f32[256,256]{1,0:T(8,128)}), f32[128,256]{1,0:T(8,128)}) %reduce-scatter.4.cloned.1.call-update) | async-done | bytes 131088 | tf_op jit(solution)/shard_map/reduce_scatter | solution.py:63
  116.2 0.0 copy-done
  116.2 0.0 copy-done.5
  116.2 0.0 copy-done.7
  116.2 1.8 convert_reduce_fusion
  118.0 0.2 fusion.13
  118.2 4.9 %all_gather.7 = bf16[256,256]{1,0:T(8,128)(2,1)S(1)} all-gather(bf16[128,256]{1,0:T(8,128)(2,1)S(1)} %fusion.13), channel_id=1, replica_groups=mesh['blk'=16,'rep'=2] {'rep'}, dimensions={0}, use_global_device_ids=true | all-gather | bytes 196608 | tf_op jit(solution)/shard_map/all_gather | solution.py:78
  123.2 5.6 %fusion.14 = bf16[128,128,256]{2,0,1:T(8,128)(2,1)} fusion(bf16[2,128,256]{2,1,0:T(8,128)(2,1)S(1)} %bitcast.42, s32[128]{0:T(128)S(1)} %eq.14), kind=kOutput, calls=%fused_computation.17 | convolution fusion | flops 16777472 | bytes 8520192 | tf_op jit(solution)/shard_map/tb,bjf->tjf/dot_general | solution.py:95
  128.8 16.7 %fusion.5 = f32[128,256,128]{2,1,0:T(8,128)} fusion(bf16[128,128,128]{2,1,0:T(8,128)(2,1)} %bitcast.38, bf16[128,128,256]{2,0,1:T(8,128)(2,1)} %fusion.14), kind=kOutput, calls=%fused_computation.7 | convolution fusion | flops 1073741824 | bytes 29360128 | tf_op jit(solution)/shard_map/tji,tjf->tif/dot_general | solution.py:98
  145.5 17.7 %copy.27 = f32[128,256,128]{1,0,2:T(8,128)} copy(f32[128,256,128]{2,1,0:T(8,128)} %fusion.5) | data formatting | bytes 33554432 | tf_op jit(solution)/shard_map/tji,tjf->tif/dot_general | solution.py:98
  163.2 0.0 copy-start.6
  163.2 0.0 copy-start.1
  163.2 9.8 %fusion.8 = bf16[32,128,256]{2,0,1:T(8,128)(2,1)S(1)} fusion(f32[128,256,128]{1,0,2:T(8,128)} %copy.27, s32[128]{0:T(128)S(1)} %and_select_fusion, pred[128]{0:T(512)(128)(4,1)S(1)} %fusion.28), kind=kOutput, calls=%fused_computation.10 | convolution fusion | flops 1611669504 | bytes 18875008 | tf_op jit(solution)/shard_map/tb,tif->bif/dot_general | solution.py:100
  173.1 2.5 copy.21
  175.6 0.0 reduce-scatter.6.cloned.1.call-update
  175.6 0.0 reduce-scatter.8.cloned.1.call-start
  175.7 61.6 %reduce-scatter.6.cloned.1.call-done = bf16[256,256]{1,0:T(8,128)(2,1)} async-done(((bf16[4096,256]{1,0:T(8,128)(2,1)}), bf16[256,256]{1,0:T(8,128)(2,1)}) %reduce-scatter.6.cloned.1.call-update) | async-done | bytes 131088 | tf_op jit(solution)/shard_map/reduce_scatter | solution.py:101
  237.3 0.0 reduce-scatter.8.cloned.1.call-update
  237.3 0.0 all-reduce.3.cloned.1.call-start
  237.4 0.9 fusion.16
  238.3 0.0 copy-done.6
  238.3 1.0 fusion.35
  239.3 0.0 all-reduce.3.cloned.1.call-update
  239.3 40.2 %psum.23 = f32[256]{0:T(256)} all-reduce(f32[256]{0:T(256)S(1)} %get-tuple-element.7), channel_id=1, replica_groups=mesh['blk'=16,'rep'=2] {'blk','rep'}, use_global_device_ids=true, to_apply=%region_6.7 | all-reduce | flops 256 | bytes 2048 | tf_op jit(solution)/shard_map/psum | solution.py:79
  279.5 0.0 reduce-scatter.8.cloned.1.call-done
  279.5 1.7 fusion.12
  281.2 101.6 %all-reduce.3.cloned.1.call-done = (f32[256,256]{1,0:T(8,128)}, f32[256,256]{1,0:T(8,128)}) async-done(((f32[256,256]{1,0:T(8,128)}, f32[256,256]{1,0:T(8,128)}), (f32[256,256]{1,0:T(8,128)}, f32[256,256]{1,0:T(8,128)})) %all-reduce.3.cloned.1.call-update) | async-done | bytes 524304 | tf_op jit(solution)/shard_map/psum | solution.py:79
  382.8 1.7 copy.38
  384.4 1.7 copy.39
  386.1 0.0 copy-done.1
  (4 shorter events, 0.0 us)
Async XLA Ops:
  7.2 109.0 %copy-start = (bf16[256,256]{1,0:T(8,128)(2,1)S(1)}, bf16[256,256]{1,0:T(8,128)(2,1)}, u32[]{:S(2)}) copy-start(bf16[256,256]{1,0:T(8,128)(2,1)} %param.17) | copy-start | bytes 393220
  7.2 47.1 %all-gather.2.cloned.1.call-start = ((), (), s32[]{:S(2)}) async-start(), calls=%async_computation.3 | async-start | bytes 2228224 | tf_op jit(solution)/shard_map/all_gather | solution.py:44
  7.9 108.3 %reduce-scatter.4.cloned.1.call-start = ((), (), s32[]{:S(2)}) async-start(), calls=%async_computation.4 | async-start | bytes 393216 | tf_op jit(solution)/shard_map/reduce_scatter | solution.py:63
  95.7 10.1 %copy-start.4 = (s32[256]{0:T(256)S(1)}, s32[256]{0:T(256)}, u32[]{:S(2)}) copy-start(s32[256]{0:T(256)} %param.11) | copy-start | bytes 3076
  95.7 10.2 %copy-start.2 = (bf16[256,256]{1,0:T(8,128)(2,1)S(1)}, bf16[256,256]{1,0:T(8,128)(2,1)}, u32[]{:S(2)}) copy-start(bf16[256,256]{1,0:T(8,128)(2,1)} %param.16) | copy-start | bytes 393220
  95.7 10.2 %copy-start.3 = (bf16[256,256]{1,0:T(8,128)(2,1)S(1)}, bf16[256,256]{1,0:T(8,128)(2,1)}, u32[]{:S(2)}) copy-start(bf16[256,256]{1,0:T(8,128)(2,1)} %param.10) | copy-start | bytes 393220
  95.7 20.5 %copy-start.5 = (bf16[256,256]{1,0:T(8,128)(2,1)S(1)}, bf16[256,256]{1,0:T(8,128)(2,1)}, u32[]{:S(2)}) copy-start(bf16[256,256]{1,0:T(8,128)(2,1)} %param.19) | copy-start | bytes 393220
  95.8 20.5 %copy-start.7 = (f32[256]{0:T(256)S(1)}, f32[256]{0:T(256)}, u32[]{:S(2)}) copy-start(f32[256]{0:T(256)} %param.18) | copy-start | bytes 3076
  105.6 131.7 %reduce-scatter.6.cloned.1.call-start = ((), (), s32[]{:S(2)}) async-start(), calls=%async_computation.5 | async-start | bytes 2228224 | tf_op jit(solution)/shard_map/reduce_scatter | solution.py:101
  163.2 75.0 %copy-start.6 = (f32[128,256]{1,0:T(8,128)S(1)}, f32[128,256]{1,0:T(8,128)}, u32[]{:S(2)}) copy-start(f32[128,256]{1,0:T(8,128)} %reduce-scatter.4.cloned.1.call-done) | copy-start | bytes 393220
  163.2 222.8 %copy-start.1 = (bf16[256,256]{1,0:T(8,128)(2,1)S(1)}, bf16[256,256]{1,0:T(8,128)(2,1)}, u32[]{:S(2)}) copy-start(bf16[256,256]{1,0:T(8,128)(2,1)} %param.17) | copy-start | bytes 393220
  175.6 103.8 %reduce-scatter.8.cloned.1.call-start = ((), (), s32[]{:S(2)}) async-start(), calls=%async_computation.6 | async-start | bytes 196608 | tf_op jit(solution)/shard_map/reduce_scatter | solution.py:104
  237.3 145.4 %all-reduce.3.cloned.1.call-start = ((), (), s32[]{:S(2)}) async-start(), calls=%async_computation.7 | async-start | bytes 1048576 | tf_op jit(solution)/shard_map/psum | solution.py:79
Sparse Core Ops, SparseCore 0:
  10.2 44.0 all-gather.1
  105.7 10.4 reduce-scatter.3
  175.7 61.4 reduce-scatter.5
  239.4 9.5 reduce-scatter.7
  254.9 127.8 all-reduce.2
where the time goes:
time: 394 us; the launch traced here: 393 us
  waiting for transfers between devices  218 us (55%)
  matrix products  70.8 us (18%)
  blocking collectives  45.1 us (11%)
  local copies, waits for them, and re-layouts  43.4 us (11%)
  between operations  13.9 us (4%)
    psum x1, waiting for transfers between devices, shards(): lax.psum((jnp.einsum('nd,ne->de', x_mine, dpre, preferred_element_type=jn...  102 us
    reduce_scatter x1, waiting for transfers between devices, shards(): lax.psum_scatter(added.reshape(count, width).astype(jnp.bfloat16), 'blk',...  61.6 us
    all_gather x1, waiting for transfers between devices, shards(): piece = lax.all_gather(features, 'blk', axis=0, tiled=True)  43.6 us
    psum x1, blocking collectives, shards(): lax.psum((jnp.einsum('nd,ne->de', x_mine, dpre, preferred_element_type=jn...  40.2 us
    dot_general x1, local copies, waits for them, and re-layouts, shards(): jnp.einsum('tji,tjf->tif', tile_sel, picked, preferred_element_type=jnp.f...  17.7 us
    dot_general x1, local copies, waits for them, and re-layouts, shards(): jnp.einsum('tij,tjf->tif', tile_sel, picked, preferred_element_type=jnp.f...  17.7 us
    dot_general x1, matrix products, shards(): jnp.einsum('tji,tjf->tif', tile_sel, picked, preferred_element_type=jnp.f...  16.7 us
    dot_general x1, matrix products, shards(): jnp.einsum('tij,tjf->tif', tile_sel, picked, preferred_element_type=jnp.f...  16.5 us
  transfers between devices with their start and end apart: 5, of which 4 were waited for; matrix products, arithmetic and copies ran while one was open for 2% of the time, Pallas kernels for 0%

commit v1 on v0

v1 whole, which is shorter than its diff:
```python
import functools

import jax
import jax.numpy as jnp
from jax import lax
from jax.experimental import pallas as pl
from jax.experimental.pallas import tpu as pltpu
from jax.sharding import PartitionSpec as P

BF = jnp.bfloat16
F32 = jnp.float32
MESH = pl.DeviceIdType.MESH
NT = (((1,), (1,)), ((), ()))
ROWS = 16
STRIP = 32


def split_rows(share):
    units = share // ROWS
    side = max(1, units * 3 // 8)
    sizes = [side, units - 2 * side, side]
    orders = ["oir", "iro", "roi"]
    parts, at = [], 0
    for size, order in zip(sizes, orders):
        if size > 0:
            parts.append((at * ROWS, size * ROWS, order))
            at += size
    return parts


def slot_shapes(parts, sizes, width):
    shapes = []
    for _, rows, order in parts:
        left = dict(sizes)
        for axis in reversed(order):
            peers = left.pop(axis) - 1
            shapes.append((peers,) + tuple(left[a] for a in "oir" if a in left) + (rows, width))
    return shapes


class Wire:
    def __init__(self, send, recv):
        self.send, self.recv, self.copies = send, recv, []

    def copy(self, src, dst, device):
        k = len(self.copies)
        c = pltpu.make_async_remote_copy(
            src_ref=src, dst_ref=dst, send_sem=self.send.at[k], recv_sem=self.recv.at[k],
            device_id=device, device_id_type=MESH,
        )
        c.start()
        self.copies.append(c)
        return c


def kernel(
    sizes, parts, nslab, cap, tile, width, slab, share,
    x_ref, deg_ref, tiles_ref, rows_ref, cols_ref, live_ref, ws_ref, wn_ref, bias_ref, cot_ref,
    hid_ref, fg_ref, gs_ref, gn_ref, gb_ref,
    tv, a_v, at_v, xg, part_v, xw, degc, xt, aggp, aggs, aggr, dg, core_in, selfp,
    g_v, g_core, g_in, g_out, g_rep, ga, b_core, b_in, b_out, b_rep,
    send_sem, recv_sem, local_sem, *slots,
):
    n_o, n_i, n_r = sizes["o"], sizes["i"], sizes["r"]
    nb = slab // tile
    blk = lax.axis_index("blk")
    rep = lax.axis_index("rep")
    core = lax.rem(blk, 2)
    sib = 1 - core
    me = {"o": blk // (2 * n_i), "i": lax.rem(blk // 2, n_i), "r": rep}
    wire = Wire(send_sem, recv_sem)

    def device(axis, to):
        at = dict(me)
        at[axis] = to
        return ((at["o"] * n_i + at["i"]) * 2 + core, at["r"])

    sibling = ((me["o"] * n_i + me["i"]) * 2 + sib, rep)

    def peers(axis):
        for k in range(1, sizes[axis]):
            to = lax.rem(me[axis] + k, sizes[axis])
            yield k, to, device(axis, to)

    load = pltpu.make_async_copy(tiles_ref.at[0, 0], tv, local_sem)
    load.start()

    mine = pl.multiple_of(rep * share, share)
    x_mine = x_ref[pl.ds(mine, share), :]
    xg[me["o"], me["i"], core, rep] = x_mine

    barrier = pltpu.get_barrier_semaphore()
    everyone = [sibling] + [d for axis in "oir" for _, _, d in peers(axis)]
    for d in everyone:
        pl.semaphore_signal(barrier, inc=1, device_id=d, device_id_type=MESH)
    pl.semaphore_wait(barrier, len(everyone))

    def box(ref, have, start, rows, core_at, fixed=None):
        at = [slice(None) if a in have else me[a] for a in "oir"]
        if fixed is not None:
            at["oir".index(fixed[0])] = fixed[1]
        return (at[0], at[1], core_at, at[2], pl.ds(start, rows), slice(None))

    def gather_stage(n):
        sent = []
        for start, rows, order in parts:
            at = box(xg, order[:n], start, rows, core)
            sent.append([wire.copy(xg.at[at], xg.at[at], d) for _, _, d in peers(order[n])])
        return sent

    flying = gather_stage(0)

    load.wait()

    def build(s, carry):
        live = live_ref[0, 0, s]
        weights = []
        for c in range(cap):
            row, col = rows_ref[0, 0, s, c], cols_ref[0, 0, s, c]
            used = c < live
            weights.append([
                [jnp.where(used & (row == i) & (col == j), 1.0, 0.0).astype(F32) for j in range(nb)]
                for i in range(nb)
            ])
        for r0 in range(0, tile, STRIP):
            acc = [[jnp.zeros((STRIP, tile), F32) for _ in range(nb)] for _ in range(nb)]
            for c in range(cap):
                t = tv[s, c, r0:r0 + STRIP, :].astype(F32)
                for i in range(nb):
                    for j in range(nb):
                        acc[i][j] = acc[i][j] + t * weights[c][i][j]
            for i in range(nb):
                for j in range(nb):
                    a_v[s, i * tile + r0:i * tile + r0 + STRIP, j * tile:(j + 1) * tile] = acc[i][j].astype(BF)
        at_v[s] = a_v[s].T
        return carry

    half = nslab // 2
    lax.fori_loop(0, half, build, 0)

    for group in flying:
        for c in group:
            c.wait_recv()
    flying = gather_stage(1)

    lax.fori_loop(half, nslab, build, 0)
    xw[...] = jnp.dot(x_mine, ws_ref[...], preferred_element_type=F32)
    xt[...] = x_mine.T
    degf = deg_ref[...].astype(F32).reshape(1, slab)
    degc[...] = jnp.broadcast_to(degf, (128, slab)).T

    for group in flying:
        for c in group:
            c.wait_recv()
    flying = gather_stage(2)
    across = []
    for group, (start, rows, order) in zip(flying, parts):
        for c in group:
            c.wait_recv()
        at = box(xg, "oir", start, rows, core)
        across.append(wire.copy(xg.at[at], xg.at[at], sibling))

    def forward(core_at):
        acc = None
        for o in range(n_o):
            for i in range(n_i):
                s = (o * n_i + i) * 2 + core_at
                d = jnp.dot(a_v[s], xg[o, i, core_at].reshape(slab, width), preferred_element_type=F32)
                acc = d if acc is None else acc + d
        return acc

    aggp[...] = forward(core)
    for c in across:
        c.wait_recv()
    aggp[...] = aggp[...] + forward(sib)

    aggs[...] = aggp[...].astype(BF).reshape(n_r, share, width)
    flying = [wire.copy(aggs.at[to], aggr.at[k - 1], d) for k, to, d in peers("r")]
    agg_sum = aggp[pl.ds(mine, share), :]
    for c in flying:
        c.wait_recv()
    for k in range(1, n_r):
        agg_sum = agg_sum + aggr[k - 1].astype(F32)
    degm = degc[pl.ds(mine, share), :]
    deg = jnp.concatenate([degm] * (width // 128), axis=1)
    agg = (agg_sum / deg).astype(BF)
    pre = xw[...] + jnp.dot(agg, wn_ref[...], preferred_element_type=F32) + bias_ref[...].reshape(1, width)
    sig = jax.nn.sigmoid(pre)
    hid_ref[...] = (pre * sig).astype(BF)
    cot = cot_ref[pl.ds(mine, share), :].astype(F32)
    dpre = (cot * (sig * (1.0 + pre * (1.0 - sig)))).astype(BF)
    dagg = lax.dot_general(dpre, wn_ref[...], NT, preferred_element_type=F32) / deg
    dg[rep] = dagg.astype(BF)
    flying = [wire.copy(dg.at[rep], dg.at[rep], d) for _, _, d in peers("r")]

    piece = g_v.shape[1:-1]
    g_v[0] = jnp.dot(xt[...], dpre, preferred_element_type=F32).astype(BF).reshape(piece + (width,))
    g_v[1] = jnp.dot(agg.T, dpre, preferred_element_type=F32).astype(BF).reshape(piece + (width,))
    grads = [wire.copy(g_v.at[sib], g_core, sibling)]
    bias_sum = jnp.sum(dpre.astype(F32), axis=0, keepdims=True)
    b_core[core] = jnp.broadcast_to(bias_sum, (8, width))
    biases = [wire.copy(b_core.at[core], b_core.at[core], sibling)]
    selfp[...] = lax.dot_general(dpre, ws_ref[...], NT, preferred_element_type=F32)

    for c in flying:
        c.wait_recv()
    dgs = dg[...].reshape(slab, width)

    def backward(o, i, core_at):
        s = (o * n_i + i) * 2 + core_at
        return jnp.dot(at_v[s], dgs, preferred_element_type=F32)

    across = []
    for o in range(n_o):
        for i in range(n_i):
            part_v[o, i, sib] = backward(o, i, sib).astype(BF).reshape(n_r, share, width)
        across.append(wire.copy(part_v.at[o, :, sib], core_in.at[o], sibling))

    def bias_stage(b_ref, at, axis):
        b_ref[at] = bias_total[0]
        return [wire.copy(b_ref.at[at], b_ref.at[at], d) for _, _, d in peers(axis)]

    bias_total = [None]

    def bias_add(copies, b_ref, n):
        for c in copies:
            c.wait_recv()
        total = b_ref[0]
        for k in range(1, n):
            total = total + b_ref[k]
        bias_total[0] = total

    bias_add(biases, b_core, 2)
    grads[0].wait_recv()
    g_v[core] = (g_v[core].astype(F32) + g_core[...].astype(F32)).astype(BF)
    grads = [wire.copy(g_v.at[core, to], g_in.at[k - 1], d) for k, to, d in peers("i")]
    biases = bias_stage(b_in, me["i"], "i")

    for o in range(n_o):
        across[o].wait_recv()
        for i in range(n_i):
            total = backward(o, i, core) + core_in[o, i].astype(F32).reshape(slab, width)
            part_v[o, i, core] = total.astype(BF).reshape(n_r, share, width)

    def scatter_stage(n):
        sent = []
        for p, (start, rows, order) in enumerate(parts):
            axis = order[2 - n]
            sent.append([
                wire.copy(
                    part_v.at[box(part_v, order[:2 - n], start, rows, core, (axis, to))],
                    slots[3 * p + n].at[k - 1], d,
                )
                for k, to, d in peers(axis)
            ])
        return sent

    def scatter_add(n, sent):
        for p, (start, rows, order) in enumerate(parts):
            at = box(part_v, order[:2 - n], start, rows, core)
            total = part_v[at].astype(F32)
            for k, c in enumerate(sent[p]):
                c.wait_recv()
                total = total + slots[3 * p + n][k].astype(F32)
            if n < 2:
                part_v[at] = total.astype(BF)
            else:
                fg_ref[start:start + rows, :] = (selfp[start:start + rows, :] + total).astype(BF)

    sent = scatter_stage(0)

    for c in grads:
        c.wait_recv()
    total = g_v[core, me["i"]].astype(F32)
    for k in range(1, n_i):
        total = total + g_in[k - 1].astype(F32)
    g_v[core, me["i"]] = total.astype(BF)
    grads = [wire.copy(g_v.at[core, me["i"], to], g_out.at[k - 1], d) for k, to, d in peers("o")]
    bias_add(biases, b_in, n_i)
    biases = bias_stage(b_out, me["o"], "o")

    scatter_add(0, sent)
    sent = scatter_stage(1)

    for c in grads:
        c.wait_recv()
    total = g_v[core, me["i"], me["o"]].astype(F32)
    for k in range(1, n_o):
        total = total + g_out[k - 1].astype(F32)
    g_rep[rep] = total.astype(BF)
    grads = [wire.copy(g_rep.at[rep], g_rep.at[rep], d) for _, _, d in peers("r")]
    bias_add(biases, b_out, n_o)
    biases = bias_stage(b_rep, rep, "r")

    scatter_add(1, sent)
    sent = scatter_stage(2)

    for c in grads:
        c.wait_recv()
    total = g_rep[0].astype(F32)
    for k in range(1, n_r):
        total = total + g_rep[k].astype(F32)
    at = (core, me["i"], me["o"])
    ga[at] = total.astype(BF)
    grads = [wire.copy(ga.at[at], ga.at[at], d) for _, _, d in peers("o")]
    bias_add(biases, b_rep, n_r)
    gb_ref[...] = bias_total[0][0:1, :].reshape(width)

    for c in grads:
        c.wait_recv()
    at = (core, me["i"])
    grads = [wire.copy(ga.at[at], ga.at[at], d) for _, _, d in peers("i")]

    scatter_add(2, sent)

    for c in grads:
        c.wait_recv()
    last = wire.copy(ga.at[core], ga.at[core], sibling)
    last.wait_recv()
    gs_ref[...] = ga[0].astype(F32).reshape(width, width)
    gn_ref[...] = ga[1].astype(F32).reshape(width, width)

    for c in wire.copies:
        c.wait_send()


def shards(n_blk, n_rep, features, degree, tiles, block_rows, block_cols, live, w_self, w_neigh, bias, cotangent):
    _, _, nslab, cap, tile, _ = tiles.shape
    slab, width = features.shape
    share = slab // n_rep
    n_i = 2
    n_o = n_blk // (2 * n_i)
    sizes = {"o": n_o, "i": n_i, "r": n_rep}
    parts = split_rows(share)
    grows = width // (n_i * n_o)
    nodes = (n_o, n_i, 2, n_rep, share, width)
    ncopy = 8 + (len(parts) + 1) * 2 * (n_o + n_i + n_rep) + n_o * 3 + n_i * 3 + n_rep * 4
    vmem = pl.BlockSpec(memory_space=pltpu.VMEM)
    smem = pl.BlockSpec(memory_space=pltpu.SMEM)
    scratch = [
        pltpu.VMEM((nslab, cap, tile, tile), BF),
        pltpu.VMEM((nslab, slab, slab), BF),
        pltpu.VMEM((nslab, slab, slab), BF),
        pltpu.VMEM(nodes, BF),
        pltpu.VMEM(nodes, BF),
        pltpu.VMEM((share, width), F32),
        pltpu.VMEM((slab, 128), F32),
        pltpu.VMEM((width, share), BF),
        pltpu.VMEM((slab, width), F32),
        pltpu.VMEM((n_rep, share, width), BF),
        pltpu.VMEM((max(1, n_rep - 1), share, width), BF),
        pltpu.VMEM((n_rep, share, width), BF),
        pltpu.VMEM((n_o, n_i, n_rep, share, width), BF),
        pltpu.VMEM((share, width), F32),
        pltpu.VMEM((2, n_i, n_o, grows, width), BF),
        pltpu.VMEM((n_i, n_o, grows, width), BF),
        pltpu.VMEM((n_i - 1, n_o, grows, width), BF),
        pltpu.VMEM((n_o - 1, grows, width), BF),
        pltpu.VMEM((n_rep, grows, width), BF),
        pltpu.VMEM((2, n_i, n_o, grows, width), BF),
        pltpu.VMEM((2, 8, width), F32),
        pltpu.VMEM((n_i, 8, width), F32),
        pltpu.VMEM((n_o, 8, width), F32),
        pltpu.VMEM((n_rep, 8, width), F32),
        pltpu.SemaphoreType.DMA((ncopy,)),
        pltpu.SemaphoreType.DMA((ncopy,)),
        pltpu.SemaphoreType.DMA,
    ] + [pltpu.VMEM(s, BF) for s in slot_shapes(parts, sizes, width)]
    return pl.pallas_call(
        functools.partial(kernel, sizes, parts, nslab, cap, tile, width, slab, share),
        out_shape=(
            jax.ShapeDtypeStruct((share, width), BF),
            jax.ShapeDtypeStruct((share, width), BF),
            jax.ShapeDtypeStruct((width, width), F32),
            jax.ShapeDtypeStruct((width, width), F32),
            jax.ShapeDtypeStruct((width,), F32),
        ),
        in_specs=[vmem, vmem, pl.BlockSpec(memory_space=pl.ANY), smem, smem, smem, vmem, vmem, vmem, vmem],
        out_specs=(vmem,) * 5,
        scratch_shapes=scratch,
        compiler_params=pltpu.CompilerParams(
            collective_id=0, has_side_effects=True, vmem_limit_bytes=56 * 1024 * 1024
        ),
        cost_estimate=pl.CostEstimate(
            flops=4 * slab * nslab * slab * width, bytes_accessed=2 * tiles.size, transcendentals=share * width
        ),
        name="sage_layer",
    )(features, degree, tiles, block_rows, block_cols, live, w_self, w_neigh, bias, cotangent)


def solution(mesh):
    n_blk, n_rep = mesh.shape["blk"], mesh.shape["rep"]
    return jax.shard_map(
        functools.partial(shards, n_blk, n_rep),
        mesh=mesh,
        in_specs=(
            P("blk", None),
            P("blk"),
            P("blk", "rep", None, None, None, None),
            P("blk", "rep", None, None),
            P("blk", "rep", None, None),
            P("blk", "rep", None),
            P(),
            P(),
            P(),
            P("blk", None),
        ),
        out_specs=(P(("blk", "rep"), None), P(("blk", "rep"), None), P(), P(), P()),
        check_vma=False,
    )
```

time: 394 us -> 70 us (0.18)
  waiting for transfers between devices: 218 us -> 0 us
  matrix products: 70.8 us -> 0 us
  Pallas kernels: 0 us -> 58.8 us
  blocking collectives: 45.1 us -> 0 us
  local copies, waits for them, and re-layouts: 43.4 us -> 10.2 us
  between operations: 13.9 us -> 0.64 us
    psum x1 -> x0, waiting for transfers between devices: 102 us -> none  [shards(): lax.psum((jnp.einsum('nd,ne->de', x_mine, dpre, preferred_element_type=jn...]
    reduce_scatter x3 -> x0, waiting for transfers between devices: 71.7 us -> none  [the longest x1 61.6 us: shards(): lax.psum_scatter(added.reshape(count, width).astype(jnp.bfloat16), 'blk',...]
    dot_general x12 -> x0, matrix products: 70.8 us -> none  [the longest x1 16.7 us: shards(): jnp.einsum('tji,tjf->tif', tile_sel, picked, preferred_element_type=jnp.f...]
    pallas_call x0 -> x1, Pallas kernels: none -> 58.8 us  [shards(): pl.pallas_call(functools.partial(kernel, sizes, parts, nslab, cap, tile,...]
    all_gather x1 -> x0, waiting for transfers between devices: 43.6 us -> none  [shards(): piece = lax.all_gather(features, 'blk', axis=0, tiled=True)]
    psum x1 -> x0, blocking collectives: 40.2 us -> none  [shards(): lax.psum((jnp.einsum('nd,ne->de', x_mine, dpre, preferred_element_type=jn...]
    dot_general x3 -> x0, local copies, waits for them, and re-layouts: 36.1 us -> none  [the longest x1 17.7 us: shards(): jnp.einsum('tji,tjf->tif', tile_sel, picked, preferred_element_type=jnp.f...]
    unnamed x19 -> x7, local copies, waits for them, and re-layouts: 4.14 us -> 10.2 us
  transfers between devices with their start and end apart: 5 -> 0, of which waited for: 4 -> 0; matrix products, arithmetic and copies ran while one was open for 2% -> 0% of each run, Pallas kernels for 0% -> 0%
where the time goes in v1:
time: 70 us; the launch traced here: 69.6 us
  Pallas kernels  58.8 us (84%)
  local copies, waits for them, and re-layouts  10.2 us (15%)
    pallas_call x1, Pallas kernels, shards(): pl.pallas_call(functools.partial(kernel, sizes, parts, nslab, cap, tile,...  58.8 us
    unnamed x7, local copies, waits for them, and re-layouts  10.2 us

profile of v1, /device:TPU:0, one launch (start us, length us, event | category | flops | bytes accessed | tf_op | source)
XLA Modules:
  0.0 69.6 jit_solution(235746338565066231)
XLA Ops:
  0.6 1.4 %copy.15.rows_ref = s32[1,1,16,8]{3,2,1,0:T(8,128)} copy(s32[1,1,16,8]{2,3,1,0:T(8,128)} %param.13) | data formatting | bytes 1024 | tf_op args[3]
  2.0 1.4 %copy.16.cols_ref = s32[1,1,16,8]{3,2,1,0:T(8,128)} copy(s32[1,1,16,8]{2,3,1,0:T(8,128)} %param.14) | data formatting | bytes 1024 | tf_op args[4]
  3.3 58.8 %sage_layer.1 = (bf16[128,256]{1,0:T(8,128)(2,1)}, bf16[128,256]{1,0:T(8,128)(2,1)}, f32[256,256]{1,0:T(8,128)}, f32[256,256]{1,0:T(8,128)}, f32[256]{0:T(256)}) custom-call(bf16[256,256]{1,0:T(8,128)(2,1)} %x_ref.1, s32[256]{0:T(256)} %deg_ref.1, bf16[1,1,16,8,128,128]{5,4,3,2,1,0:T(8,128)(2,1)} %tiles_ref.1, s32[1,1,16,8]{3,2,1,0:T(8,128)} %copy.15.rows_ref, ...), custom_call_target="tpu_custom_call" | custom-call | flops 1073741824 | bytes 4194304 | tf_op jit(solution)/shard_map/sage_layer/pallas_call | solution.py:369
  62.1 1.5 %copy.22 = bf16[128,256]{1,0:T(8,128)(2,1)} copy(bf16[128,256]{1,0:T(8,128)(2,1)} %get-tuple-element.10) | data formatting | bytes 131072
  63.6 1.5 %copy.23 = bf16[128,256]{1,0:T(8,128)(2,1)} copy(bf16[128,256]{1,0:T(8,128)(2,1)} %get-tuple-element.11) | data formatting | bytes 131072
  65.1 1.7 %copy.24 = f32[256,256]{1,0:T(8,128)} copy(f32[256,256]{1,0:T(8,128)} %get-tuple-element.12) | data formatting | bytes 524288
  66.8 1.7 %copy.25 = f32[256,256]{1,0:T(8,128)} copy(f32[256,256]{1,0:T(8,128)} %get-tuple-element.13) | data formatting | bytes 524288
  68.4 1.2 %copy.26 = f32[256]{0:T(256)} copy(f32[256]{0:T(256)} %get-tuple-element.14) | data formatting | bytes 2048

commit v2 on v1

v2 whole, which is shorter than its diff:
```python
import functools

import jax
import jax.numpy as jnp
from jax import lax
from jax.experimental import pallas as pl
from jax.experimental.pallas import tpu as pltpu
from jax.sharding import PartitionSpec as P

BF = jnp.bfloat16
F32 = jnp.float32
MESH = pl.DeviceIdType.MESH
NT = (((1,), (1,)), ((), ()))
ROWS = 16
STRIP = 32


def split_rows(share):
    units = share // ROWS
    side = max(1, units * 3 // 8)
    sizes = [side, units - 2 * side, side]
    orders = ["oir", "iro", "roi"]
    parts, at = [], 0
    for size, order in zip(sizes, orders):
        if size > 0:
            parts.append((at * ROWS, size * ROWS, order))
            at += size
    return parts


def slot_shapes(parts, sizes, width):
    shapes = []
    for _, rows, order in parts:
        left = dict(sizes)
        for axis in reversed(order):
            peers = left.pop(axis) - 1
            shapes.append((peers,) + tuple(left[a] for a in "oir" if a in left) + (rows, width))
    return shapes


class Wire:
    def __init__(self, send, recv):
        self.send, self.recv, self.copies = send, recv, []

    def copy(self, src, dst, device):
        k = len(self.copies)
        c = pltpu.make_async_remote_copy(
            src_ref=src, dst_ref=dst, send_sem=self.send.at[k], recv_sem=self.recv.at[k],
            device_id=device, device_id_type=MESH,
        )
        c.start()
        self.copies.append(c)
        return c


def kernel(
    sizes, parts, nslab, cap, tile, width, slab, share,
    x_ref, deg_ref, tiles_ref, rows_ref, cols_ref, live_ref, ws_hbm, wn_hbm, bias_ref, cot_hbm,
    hid_ref, fg_ref, ga, gb_ref,
    tv, a_v, at_v, xg, part_v, xw, degc, xt, aggp, aggs, aggr, dg, core_in, selfp,
    g_v, g_core, g_chip, g_rep, b_core, b_chip, b_rep, ws_v, wn_v, cot_v,
    send_sem, recv_sem, local_sem, *slots,
):
    n_o, n_i, n_r = sizes["o"], sizes["i"], sizes["r"]
    nb = slab // tile
    blk = lax.axis_index("blk")
    rep = lax.axis_index("rep")
    core = lax.rem(blk, 2)
    sib = 1 - core
    me = {"o": blk // (2 * n_i), "i": lax.rem(blk // 2, n_i), "r": rep}
    wire = Wire(send_sem, recv_sem)

    def device(axis, to):
        at = dict(me)
        at[axis] = to
        return ((at["o"] * n_i + at["i"]) * 2 + core, at["r"])

    sibling = ((me["o"] * n_i + me["i"]) * 2 + sib, rep)

    def peers(axis):
        for k in range(1, sizes[axis]):
            to = lax.rem(me[axis] + k, sizes[axis])
            yield k, to, device(axis, to)

    n_c = n_o * n_i
    chip = blk // 2

    def chips():
        for k in range(1, n_c):
            to = lax.rem(chip + k, n_c)
            yield k, to, (to * 2 + core, rep)

    loads = [
        pltpu.make_async_copy(src, dst, local_sem.at[k])
        for k, (src, dst) in enumerate(
            [(tiles_ref.at[0, 0], tv), (ws_hbm, ws_v), (wn_hbm, wn_v), (cot_hbm, cot_v)]
        )
    ]
    for c in loads:
        c.start()

    mine = pl.multiple_of(rep * share, share)
    x_mine = x_ref[pl.ds(mine, share), :]
    xg[me["o"], me["i"], core, rep] = x_mine
    for start, rows, order in parts:
        if order[0] == "r":
            for k in range(n_r):
                at = k * share + start
                xg[me["o"], me["i"], core, k, start:start + rows, :] = x_ref[at:at + rows, :]

    barrier = pltpu.get_barrier_semaphore()
    everyone = [sibling] + [d for _, _, d in chips()] + [d for _, _, d in peers("r")]
    for d in everyone:
        pl.semaphore_signal(barrier, inc=1, device_id=d, device_id_type=MESH)
    pl.semaphore_wait(barrier, len(everyone))

    def box(ref, have, start, rows, core_at, fixed=None):
        at = [slice(None) if a in have else me[a] for a in "oir"]
        if fixed is not None:
            at["oir".index(fixed[0])] = fixed[1]
        return (at[0], at[1], core_at, at[2], pl.ds(start, rows), slice(None))

    def gather(p, n):
        start, rows, order = parts[p]
        if n == 0 and order[0] == "r":
            return []
        if n == 3:
            at = box(xg, "oir", start, rows, core)
            return [wire.copy(xg.at[at], xg.at[at], sibling)]
        at = box(xg, order[:n], start, rows, core)
        return [wire.copy(xg.at[at], xg.at[at], d) for _, _, d in peers(order[n])]

    def arrived(copies):
        for c in copies:
            c.wait_recv()

    every = range(len(parts))
    lead = [p for p in every if parts[p][2][0] == "r"]
    rest = [p for p in every if p not in lead]

    flying = {p: gather(p, 0) for p in rest}
    for p in lead:
        flying[p] = gather(p, 1)

    loads[0].wait()

    def build(s, carry):
        live = live_ref[0, 0, s]
        weights = []
        for c in range(cap):
            row, col = rows_ref[0, 0, c, s], cols_ref[0, 0, c, s]
            used = c < live
            weights.append([
                [jnp.where(used & (row == i) & (col == j), 1.0, 0.0).astype(F32) for j in range(nb)]
                for i in range(nb)
            ])
        for r0 in range(0, tile, STRIP):
            acc = [[jnp.zeros((STRIP, tile), F32) for _ in range(nb)] for _ in range(nb)]
            for c in range(cap):
                t = tv[s, c, r0:r0 + STRIP, :].astype(F32)
                for i in range(nb):
                    for j in range(nb):
                        acc[i][j] = acc[i][j] + t * weights[c][i][j]
            for i in range(nb):
                for j in range(nb):
                    a_v[s, i * tile + r0:i * tile + r0 + STRIP, j * tile:(j + 1) * tile] = acc[i][j].astype(BF)
        at_v[s] = a_v[s].T
        return carry

    half = nslab // 2
    lax.fori_loop(0, half, build, 0)

    for p in reversed(rest):
        arrived(flying[p])
        flying[p] = gather(p, 1)

    lax.fori_loop(half, nslab, build, 0)
    for c in loads[1:]:
        c.wait()
    xw[...] = jnp.dot(x_mine, ws_v[...], preferred_element_type=F32)
    xt[...] = x_mine.T
    degf = deg_ref[...].astype(F32).reshape(1, slab)
    degc[...] = jnp.broadcast_to(degf, (128, slab)).T

    for p in list(reversed(rest)) + lead:
        arrived(flying[p])
        flying[p] = gather(p, 2)
    for p in rest[:1] + lead + rest[1:]:
        arrived(flying[p])
        flying[p] = gather(p, 3)

    def forward(core_at):
        acc = None
        for o in range(n_o):
            for i in range(n_i):
                s = (o * n_i + i) * 2 + core_at
                d = jnp.dot(a_v[s], xg[o, i, core_at].reshape(slab, width), preferred_element_type=F32)
                acc = d if acc is None else acc + d
        return acc

    aggp[...] = forward(core)
    for p in every:
        arrived(flying[p])
    aggp[...] = aggp[...] + forward(sib)

    aggs[...] = aggp[...].astype(BF).reshape(n_r, share, width)
    flying = [wire.copy(aggs.at[to], aggr.at[k - 1], d) for k, to, d in peers("r")]
    agg_sum = aggp[pl.ds(mine, share), :]
    for c in flying:
        c.wait_recv()
    for k in range(1, n_r):
        agg_sum = agg_sum + aggr[k - 1].astype(F32)
    degm = degc[pl.ds(mine, share), :]
    deg = jnp.concatenate([degm] * (width // 128), axis=1)
    agg = (agg_sum / deg).astype(BF)
    pre = xw[...] + jnp.dot(agg, wn_v[...], preferred_element_type=F32) + bias_ref[...].reshape(1, width)
    sig = jax.nn.sigmoid(pre)
    hid_ref[...] = (pre * sig).astype(BF)
    cot = cot_v[pl.ds(mine, share), :].astype(F32)
    dpre = (cot * (sig * (1.0 + pre * (1.0 - sig)))).astype(BF)
    dagg = lax.dot_general(dpre, wn_v[...], NT, preferred_element_type=F32) / deg
    dg[rep] = dagg.astype(BF)
    flying = [wire.copy(dg.at[rep], dg.at[rep], d) for _, _, d in peers("r")]

    piece = g_v.shape[1:-1]
    g_v[0] = jnp.dot(xt[...], dpre, preferred_element_type=F32).astype(BF).reshape(piece + (width,))
    g_v[1] = jnp.dot(agg.T, dpre, preferred_element_type=F32).astype(BF).reshape(piece + (width,))
    grads = [wire.copy(g_v.at[sib], g_core, sibling)]
    bias_sum = jnp.sum(dpre.astype(F32), axis=0, keepdims=True)
    b_core[core] = jnp.broadcast_to(bias_sum, (8, width))
    biases = [wire.copy(b_core.at[core], b_core.at[core], sibling)]
    selfp[...] = lax.dot_general(dpre, ws_v[...], NT, preferred_element_type=F32)

    for c in flying:
        c.wait_recv()
    dgs = dg[...].reshape(slab, width)

    def backward(o, i, core_at):
        s = (o * n_i + i) * 2 + core_at
        return jnp.dot(at_v[s], dgs, preferred_element_type=F32)

    across = []
    for o in range(n_o):
        for i in range(n_i):
            part_v[o, i, sib] = backward(o, i, sib).astype(BF).reshape(n_r, share, width)
        across.append(wire.copy(part_v.at[o, :, sib], core_in.at[o], sibling))

    def bias_sum_of(b_ref, n):
        total = b_ref[0]
        for k in range(1, n):
            total = total + b_ref[k]
        return total

    arrived(grads + biases)
    g_v[core] = (g_v[core].astype(F32) + g_core[...].astype(F32)).astype(BF)
    grads = [wire.copy(g_v.at[core, to], g_chip.at[k - 1], d) for k, to, d in chips()]
    b_chip[chip] = bias_sum_of(b_core, 2)
    biases = [wire.copy(b_chip.at[chip], b_chip.at[chip], d) for _, _, d in chips()]

    for o in range(n_o):
        across[o].wait_recv()
        for i in range(n_i):
            total = backward(o, i, core) + core_in[o, i].astype(F32).reshape(slab, width)
            part_v[o, i, core] = total.astype(BF).reshape(n_r, share, width)

    def scatter(p, n):
        start, rows, order = parts[p]
        axis = order[2 - n]
        return [
            wire.copy(
                part_v.at[box(part_v, order[:2 - n], start, rows, core, (axis, to))],
                slots[3 * p + n].at[k - 1], d,
            )
            for k, to, d in peers(axis)
        ]

    def scatter_add(p, n, sent):
        start, rows, order = parts[p]
        at = box(part_v, order[:2 - n], start, rows, core)
        arrived(sent)
        total = part_v[at].astype(F32)
        for k in range(len(sent)):
            total = total + slots[3 * p + n][k].astype(F32)
        if n < 2:
            part_v[at] = total.astype(BF)
        else:
            fg_ref[start:start + rows, :] = (selfp[start:start + rows, :] + total).astype(BF)

    turns = rest[:1] + lead + rest[1:]
    sent = {p: scatter(p, 0) for p in every}

    arrived(grads + biases)
    total = g_v[core, chip].astype(F32)
    for k in range(1, n_c):
        total = total + g_chip[k - 1].astype(F32)
    g_rep[rep] = total.astype(BF)
    grads = [wire.copy(g_rep.at[rep], g_rep.at[rep], d) for _, _, d in peers("r")]
    b_rep[rep] = bias_sum_of(b_chip, n_c)
    biases = [wire.copy(b_rep.at[rep], b_rep.at[rep], d) for _, _, d in peers("r")]

    for p in turns:
        scatter_add(p, 0, sent[p])
        sent[p] = scatter(p, 1)

    arrived(grads + biases)
    total = g_rep[0].astype(F32)
    for k in range(1, n_r):
        total = total + g_rep[k].astype(F32)
    ga[core, chip] = total.astype(BF)
    grads = [wire.copy(ga.at[core, chip], ga.at[core, chip], d) for _, _, d in chips()]
    gb_ref[...] = bias_sum_of(b_rep, n_r)

    for p in turns:
        scatter_add(p, 1, sent[p])
        sent[p] = scatter(p, 2)

    arrived(grads)
    last = wire.copy(ga.at[core], ga.at[core], sibling)
    for p in turns:
        scatter_add(p, 2, sent[p])
    last.wait_recv()

    for c in wire.copies:
        c.wait_send()


def finish(hid_in, fg_in, ga, gb_in, hid_ref, fg_ref, gs_ref, gn_ref, gb_ref):
    width = gs_ref.shape[0]
    hid_ref[...] = hid_in[...]
    fg_ref[...] = fg_in[...]
    gs_ref[...] = ga[0].astype(F32).reshape(width, width)
    gn_ref[...] = ga[1].astype(F32).reshape(width, width)
    gb_ref[...] = gb_in[0:1, :].reshape(width)


def shards(n_blk, n_rep, features, degree, tiles, block_rows, block_cols, live, w_self, w_neigh, bias, cotangent):
    _, _, nslab, cap, tile, _ = tiles.shape
    slab, width = features.shape
    share = slab // n_rep
    n_i = 2
    n_o = n_blk // (2 * n_i)
    sizes = {"o": n_o, "i": n_i, "r": n_rep}
    parts = split_rows(share)
    n_c = n_o * n_i
    grows = width // n_c
    nodes = (n_o, n_i, 2, n_rep, share, width)
    ncopy = 8 + (len(parts) + 1) * 2 * (n_o + n_i + n_rep) + n_o + n_c * 3 + n_rep * 4
    vmem = pl.BlockSpec(memory_space=pltpu.VMEM)
    smem = pl.BlockSpec(memory_space=pltpu.SMEM)
    scratch = [
        pltpu.VMEM((nslab, cap, tile, tile), BF),
        pltpu.VMEM((nslab, slab, slab), BF),
        pltpu.VMEM((nslab, slab, slab), BF),
        pltpu.VMEM(nodes, BF),
        pltpu.VMEM(nodes, BF),
        pltpu.VMEM((share, width), F32),
        pltpu.VMEM((slab, 128), F32),
        pltpu.VMEM((width, share), BF),
        pltpu.VMEM((slab, width), F32),
        pltpu.VMEM((n_rep, share, width), BF),
        pltpu.VMEM((max(1, n_rep - 1), share, width), BF),
        pltpu.VMEM((n_rep, share, width), BF),
        pltpu.VMEM((n_o, n_i, n_rep, share, width), BF),
        pltpu.VMEM((share, width), F32),
        pltpu.VMEM((2, n_c, grows, width), BF),
        pltpu.VMEM((n_c, grows, width), BF),
        pltpu.VMEM((n_c - 1, grows, width), BF),
        pltpu.VMEM((n_rep, grows, width), BF),
        pltpu.VMEM((2, 8, width), F32),
        pltpu.VMEM((n_c, 8, width), F32),
        pltpu.VMEM((n_rep, 8, width), F32),
        pltpu.VMEM((width, width), BF),
        pltpu.VMEM((width, width), BF),
        pltpu.VMEM((slab, width), BF),
        pltpu.SemaphoreType.DMA((ncopy,)),
        pltpu.SemaphoreType.DMA((ncopy,)),
        pltpu.SemaphoreType.DMA((4,)),
    ] + [pltpu.VMEM(s, BF) for s in slot_shapes(parts, sizes, width)]
    anywhere = pl.BlockSpec(memory_space=pl.ANY)
    done = pl.pallas_call(
        functools.partial(kernel, sizes, parts, nslab, cap, tile, width, slab, share),
        out_shape=(
            jax.ShapeDtypeStruct((share, width), BF),
            jax.ShapeDtypeStruct((share, width), BF),
            jax.ShapeDtypeStruct((2, n_c, grows, width), BF),
            jax.ShapeDtypeStruct((8, width), F32),
        ),
        in_specs=[vmem, vmem, anywhere, smem, smem, smem, anywhere, anywhere, vmem, anywhere],
        out_specs=(vmem,) * 4,
        scratch_shapes=scratch,
        compiler_params=pltpu.CompilerParams(
            collective_id=0, has_side_effects=True, vmem_limit_bytes=56 * 1024 * 1024
        ),
        cost_estimate=pl.CostEstimate(
            flops=4 * slab * nslab * slab * width, bytes_accessed=2 * tiles.size, transcendentals=share * width
        ),
        name="sage_layer",
    )(features, degree, tiles, jnp.swapaxes(block_rows, 2, 3), jnp.swapaxes(block_cols, 2, 3), live, w_self, w_neigh, bias, cotangent)
    return pl.pallas_call(
        finish,
        out_shape=(
            jax.ShapeDtypeStruct((share, width), BF),
            jax.ShapeDtypeStruct((share, width), BF),
            jax.ShapeDtypeStruct((width, width), F32),
            jax.ShapeDtypeStruct((width, width), F32),
            jax.ShapeDtypeStruct((width,), F32),
        ),
        in_specs=[vmem] * 4,
        out_specs=(vmem,) * 5,
        name="write_results",
    )(*done)


def solution(mesh):
    n_blk, n_rep = mesh.shape["blk"], mesh.shape["rep"]
    return jax.shard_map(
        functools.partial(shards, n_blk, n_rep),
        mesh=mesh,
        in_specs=(
            P("blk", None),
            P("blk"),
            P("blk", "rep", None, None, None, None),
            P("blk", "rep", None, None),
            P("blk", "rep", None, None),
            P("blk", "rep", None),
            P(),
            P(),
            P(),
            P("blk", None),
        ),
        out_specs=(P(("blk", "rep"), None), P(("blk", "rep"), None), P(), P(), P()),
        check_vma=False,
    )
```

time: 70 us -> 56.9 us (0.81)
  local copies, waits for them, and re-layouts: 10.2 us -> 0 us
  Pallas kernels: 58.8 us -> 56.1 us
    unnamed x7 -> x0, local copies, waits for them, and re-layouts: 10.2 us -> none
    pallas_call x1, Pallas kernels: 58.8 us -> 54.2 us  [shards(): pl.pallas_call(functools.partial(kernel, sizes, parts, nslab, cap, tile,...]
    pallas_call x0 -> x1, Pallas kernels: none -> 1.88 us  [shards(): pl.pallas_call(finish, out_shape=(jax.ShapeDtypeStruct((share, width), BF...]
where the time goes in v2:
time: 56.9 us; the launch traced here: 56.7 us
  Pallas kernels  56.1 us (99%)
  between operations  0.64 us (1%)
    pallas_call x1, Pallas kernels, shards(): pl.pallas_call(functools.partial(kernel, sizes, parts, nslab, cap, tile,...  54.2 us
    pallas_call x1, Pallas kernels, shards(): pl.pallas_call(finish, out_shape=(jax.ShapeDtypeStruct((share, width), BF...  1.88 us

profile of v2, /device:TPU:0, one launch (start us, length us, event | category | flops | bytes accessed | tf_op | source)
XLA Modules:
  0.0 56.7 jit_solution(5942800490246627277)
XLA Ops:
  0.6 54.2 %sage_layer.1 = (bf16[128,256]{1,0:T(8,128)(2,1)}, bf16[128,256]{1,0:T(8,128)(2,1)}, bf16[2,8,32,256]{3,2,1,0:T(8,128)(2,1)}, f32[8,256]{1,0:T(8,128)}) custom-call(bf16[256,256]{1,0:T(8,128)(2,1)} %x_ref.1, s32[256]{0:T(256)} %deg_ref.1, bf16[1,1,16,8,128,128]{5,4,3,2,1,0:T(8,128)(2,1)} %tiles_ref.1, s32[1,1,8,16]{3,2,1,0:T(8,128)} %bitcast.2, ...), custom_call_target="tpu_custom_call" | custom-call | flops 1073741824 | bytes 4194304 | tf_op jit(solution)/shard_map/sage_layer/pallas_call | solution.py:380
  54.8 1.9 %write_results.1 = (bf16[128,256]{1,0:T(8,128)(2,1)}, bf16[128,256]{1,0:T(8,128)(2,1)}, f32[256,256]{1,0:T(8,128)}, f32[256,256]{1,0:T(8,128)}, f32[256]{0:T(256)}) custom-call(bf16[128,256]{1,0:T(8,128)(2,1)} %get-tuple-element.9.hid_in, bf16[128,256]{1,0:T(8,128)(2,1)} %get-tuple-element.10.fg_in, bf16[2,8,32,256]{3,2,1,0:T(8,128)(2,1)} %get-tuple-element.11.ga, ...), custom_call_target="tpu_custom_call" | custom-call | tf_op jit(solution)/shard_map/write_results/pallas_call | solution.py:399

commit v3 on v2

--- a/solution.py
+++ b/solution.py
@@ -215,19 +215,19 @@
     agg = (agg_sum / deg).astype(BF)
     pre = xw[...] + jnp.dot(agg, wn_v[...], preferred_element_type=F32) + bias_ref[...].reshape(1, width)
     sig = jax.nn.sigmoid(pre)
-    hid_ref[...] = (pre * sig).astype(BF)
     cot = cot_v[pl.ds(mine, share), :].astype(F32)
     dpre = (cot * (sig * (1.0 + pre * (1.0 - sig)))).astype(BF)
     dagg = lax.dot_general(dpre, wn_v[...], NT, preferred_element_type=F32) / deg
     dg[rep] = dagg.astype(BF)
     flying = [wire.copy(dg.at[rep], dg.at[rep], d) for _, _, d in peers("r")]
 
+    hid_ref[...] = (pre * sig).astype(BF)
     piece = g_v.shape[1:-1]
     g_v[0] = jnp.dot(xt[...], dpre, preferred_element_type=F32).astype(BF).reshape(piece + (width,))
     g_v[1] = jnp.dot(agg.T, dpre, preferred_element_type=F32).astype(BF).reshape(piece + (width,))
     grads = [wire.copy(g_v.at[sib], g_core, sibling)]
     bias_sum = jnp.sum(dpre.astype(F32), axis=0, keepdims=True)
-    b_core[core] = jnp.broadcast_to(bias_sum, (8, width))
+    b_core[core] = bias_sum
     biases = [wire.copy(b_core.at[core], b_core.at[core], sibling)]
     selfp[...] = lax.dot_general(dpre, ws_v[...], NT, preferred_element_type=F32)
 
@@ -238,24 +238,24 @@
     def backward(o, i, core_at):
         s = (o * n_i + i) * 2 + core_at
         return jnp.dot(at_v[s], dgs, preferred_element_type=F32)
+
+    def bias_sum_of(b_ref, n):
+        total = b_ref[0]
+        for k in range(1, n):
+            total = total + b_ref[k]
+        return total
+
+    arrived(grads + biases)
+    g_v[core] = (g_v[core].astype(F32) + g_core[...].astype(F32)).astype(BF)
+    grads = [wire.copy(g_v.at[core, to], g_chip.at[k - 1], d) for k, to, d in chips()]
+    b_chip[chip] = bias_sum_of(b_core, 2)
+    biases = [wire.copy(b_chip.at[chip], b_chip.at[chip], d) for _, _, d in chips()]
 
     across = []
     for o in range(n_o):
         for i in range(n_i):
             part_v[o, i, sib] = backward(o, i, sib).astype(BF).reshape(n_r, share, width)
         across.append(wire.copy(part_v.at[o, :, sib], core_in.at[o], sibling))
-
-    def bias_sum_of(b_ref, n):
-        total = b_ref[0]
-        for k in range(1, n):
-            total = total + b_ref[k]
-        return total
-
-    arrived(grads + biases)
-    g_v[core] = (g_v[core].astype(F32) + g_core[...].astype(F32)).astype(BF)
-    grads = [wire.copy(g_v.at[core, to], g_chip.at[k - 1], d) for k, to, d in chips()]
-    b_chip[chip] = bias_sum_of(b_core, 2)
-    biases = [wire.copy(b_chip.at[chip], b_chip.at[chip], d) for _, _, d in chips()]
 
     for o in range(n_o):
         across[o].wait_recv()
@@ -308,7 +308,7 @@
         total = total + g_rep[k].astype(F32)
     ga[core, chip] = total.astype(BF)
     grads = [wire.copy(ga.at[core, chip], ga.at[core, chip], d) for _, _, d in chips()]
-    gb_ref[...] = bias_sum_of(b_rep, n_r)
+    gb_ref[...] = jnp.broadcast_to(bias_sum_of(b_rep, n_r), (8, width))
 
     for p in turns:
         scatter_add(p, 1, sent[p])
@@ -366,9 +366,9 @@
         pltpu.VMEM((n_c, grows, width), BF),
         pltpu.VMEM((n_c - 1, grows, width), BF),
         pltpu.VMEM((n_rep, grows, width), BF),
-        pltpu.VMEM((2, 8, width), F32),
-        pltpu.VMEM((n_c, 8, width), F32),
-        pltpu.VMEM((n_rep, 8, width), F32),
+        pltpu.VMEM((2, 1, width), F32),
+        pltpu.VMEM((n_c, 1, width), F32),
+        pltpu.VMEM((n_rep, 1, width), F32),
         pltpu.VMEM((width, width), BF),
         pltpu.VMEM((width, width), BF),
         pltpu.VMEM((slab, width), BF),

time: 56.9 us -> 55.8 us (0.981)
  Pallas kernels: 56.1 us -> 55 us
    pallas_call x1, Pallas kernels: 54.2 us -> 53.1 us  [shards(): pl.pallas_call(functools.partial(kernel, sizes, parts, nslab, cap, tile,...]
where the time goes in v3:
time: 55.8 us; the launch traced here: 55.6 us
  Pallas kernels  55 us (99%)
  between operations  0.64 us (1%)
    pallas_call x1, Pallas kernels, shards(): pl.pallas_call(functools.partial(kernel, sizes, parts, nslab, cap, tile,...  53.1 us
    pallas_call x1, Pallas kernels, shards(): pl.pallas_call(finish, out_shape=(jax.ShapeDtypeStruct((share, width), BF...  1.88 us

profile of v3, /device:TPU:0, one launch (start us, length us, event | category | flops | bytes accessed | tf_op | source)
XLA Modules:
  0.0 55.6 jit_solution(7364610402204850483)
XLA Ops:
  0.6 53.1 %sage_layer.1 = (bf16[128,256]{1,0:T(8,128)(2,1)}, bf16[128,256]{1,0:T(8,128)(2,1)}, bf16[2,8,32,256]{3,2,1,0:T(8,128)(2,1)}, f32[8,256]{1,0:T(8,128)}) custom-call(bf16[256,256]{1,0:T(8,128)(2,1)} %x_ref.1, s32[256]{0:T(256)} %deg_ref.1, bf16[1,1,16,8,128,128]{5,4,3,2,1,0:T(8,128)(2,1)} %tiles_ref.1, s32[1,1,8,16]{3,2,1,0:T(8,128)} %bitcast.2, ...), custom_call_target="tpu_custom_call" | custom-call | flops 1073741824 | bytes 4194304 | tf_op jit(solution)/shard_map/sage_layer/pallas_call | solution.py:380
  53.7 1.9 %write_results.1 = (bf16[128,256]{1,0:T(8,128)(2,1)}, bf16[128,256]{1,0:T(8,128)(2,1)}, f32[256,256]{1,0:T(8,128)}, f32[256,256]{1,0:T(8,128)}, f32[256]{0:T(256)}) custom-call(bf16[128,256]{1,0:T(8,128)(2,1)} %get-tuple-element.9.hid_in, bf16[128,256]{1,0:T(8,128)(2,1)} %get-tuple-element.10.fg_in, bf16[2,8,32,256]{3,2,1,0:T(8,128)(2,1)} %get-tuple-element.11.ga, ...), custom_call_target="tpu_custom_call" | custom-call | tf_op jit(solution)/shard_map/write_results/pallas_call | solution.py:399

commit v4 on v3

--- a/solution.py
+++ b/solution.py
@@ -138,9 +138,9 @@
     lead = [p for p in every if parts[p][2][0] == "r"]
     rest = [p for p in every if p not in lead]
 
-    flying = {p: gather(p, 0) for p in rest}
-    for p in lead:
-        flying[p] = gather(p, 1)
+    flying = {p: gather(p, 1) for p in lead}
+    for p in rest:
+        flying[p] = gather(p, 0)
 
     loads[0].wait()
 

time: 55.8 us -> 58.7 us (1.052)
  Pallas kernels: 55 us -> 57.9 us
    pallas_call x1, Pallas kernels: 53.1 us -> 56 us  [shards(): pl.pallas_call(functools.partial(kernel, sizes, parts, nslab, cap, tile,...]
where the time goes in v4:
time: 58.7 us; the launch traced here: 58.5 us
  Pallas kernels  57.9 us (99%)
  between operations  0.64 us (1%)
    pallas_call x1, Pallas kernels, shards(): pl.pallas_call(functools.partial(kernel, sizes, parts, nslab, cap, tile,...  56 us
    pallas_call x1, Pallas kernels, shards(): pl.pallas_call(finish, out_shape=(jax.ShapeDtypeStruct((share, width), BF...  1.88 us

profile of v4, /device:TPU:0, one launch (start us, length us, event | category | flops | bytes accessed | tf_op | source)
XLA Modules:
  0.0 58.5 jit_solution(7575121590449643021)
XLA Ops:
  0.6 56.0 %sage_layer.1 = (bf16[128,256]{1,0:T(8,128)(2,1)}, bf16[128,256]{1,0:T(8,128)(2,1)}, bf16[2,8,32,256]{3,2,1,0:T(8,128)(2,1)}, f32[8,256]{1,0:T(8,128)}) custom-call(bf16[256,256]{1,0:T(8,128)(2,1)} %x_ref.1, s32[256]{0:T(256)} %deg_ref.1, bf16[1,1,16,8,128,128]{5,4,3,2,1,0:T(8,128)(2,1)} %tiles_ref.1, s32[1,1,8,16]{3,2,1,0:T(8,128)} %bitcast.2, ...), custom_call_target="tpu_custom_call" | custom-call | flops 1073741824 | bytes 4194304 | tf_op jit(solution)/shard_map/sage_layer/pallas_call | solution.py:380
  56.6 1.9 %write_results.1 = (bf16[128,256]{1,0:T(8,128)(2,1)}, bf16[128,256]{1,0:T(8,128)(2,1)}, f32[256,256]{1,0:T(8,128)}, f32[256,256]{1,0:T(8,128)}, f32[256]{0:T(256)}) custom-call(bf16[128,256]{1,0:T(8,128)(2,1)} %get-tuple-element.9.hid_in, bf16[128,256]{1,0:T(8,128)(2,1)} %get-tuple-element.10.fg_in, bf16[2,8,32,256]{3,2,1,0:T(8,128)(2,1)} %get-tuple-element.11.ga, ...), custom_call_target="tpu_custom_call" | custom-call | tf_op jit(solution)/shard_map/write_results/pallas_call | solution.py:399
